TPU v7x, 32 devices: a whole 2x2x4 slice. The times are simulated.
32 devices in a mesh: dp: 4 (over y, x), tensor: 8 (over z, core).
Axes of the slice: x: 2, y: 2, z: 4, core: 2. Of those that a mesh axis runs over, the one named last changes fastest.
Arguments:
- query_states: bfloat16 [1536, 4096], P('dp', 'tensor'), may hold values from -64 to 64
- key_states: bfloat16 [1536, 4096], P('dp', 'tensor'), may hold values from -12 to 12
- value_states: bfloat16 [1536, 4096], P('dp', 'tensor'), may hold values from -6 to 6
- residual: bfloat16 [1536, 4096], P('dp', 'tensor'), may hold values from -6 to 6
- norm_gains: float32 [4, 4096], replicated, may hold values from 0.1 to 1.9
- lang_labels: int32 [32], replicated, may hold values from 0 to 3
- doc_lengths: int32 [32, 4], replicated, may hold values from 1 to 32, 48 in all within a row
- destinations: int32 [32], replicated, may hold values from 0 to 3, as said below
- gate_weight: bfloat16 [4096, 14336], P(None, 'tensor'), may hold values from -0.09375 to 0.09375
- up_weight: bfloat16 [4096, 14336], P(None, 'tensor'), may hold values from -0.09375 to 0.09375
- down_weight: bfloat16 [14336, 4096], P('tensor'), may hold values from -0.046875 to 0.046875
- out_cotangent: bfloat16 [1536, 4096], P(('dp', 'tensor')), may hold values from -6 to 6
Outputs:
- layer_out: bfloat16 [1536, 4096], P(('dp', 'tensor'))
- input_grad: bfloat16 [1536, 4096], P(('dp', 'tensor'))
- gate_grad: bfloat16 [4096, 14336], P('dp', 'tensor')
- up_grad: bfloat16 [4096, 14336], P('dp', 'tensor')
- down_grad: bfloat16 [14336, 4096], P('tensor', 'dp')
Inputs may be any that keep to these rules, and one draw needn't show every extreme that they name: `destinations`: every data group receives exactly 8 units. One group sends at most 2 units to any one group, and every group sends exactly 2 units to some group.
All inputs are finite; a program needn't handle non-finite values.
Results may differ from a plain program's by a relative error of at most 0.015.
Values may be sent and summed in bfloat16 or wider, within the bound.
A program may use at most 192 MiB of HBM per device.

v0:
```python
import math

import jax
import jax.numpy as jnp
from jax import lax
from jax.sharding import PartitionSpec as P

HD = 128
UNIT = 48
CAP = 2
WIN = 24


def doc_index(doc_lengths, unit_len):
    doc_ends = jnp.cumsum(doc_lengths, axis=1)
    positions = jnp.arange(unit_len, dtype=jnp.int32)
    return jnp.sum((doc_ends[:, None, :] <= positions[None, :, None]).astype(jnp.int32), axis=2)


def attend(query_units, key_units, value_units, resid_units, doc_units):
    unit_count, unit_len, columns = query_units.shape
    head_shape = (unit_count, unit_len, columns // HD, HD)
    scores = jnp.einsum(
        "uqhd,ukhd->uhqk",
        query_units.reshape(head_shape),
        key_units.reshape(head_shape),
        preferred_element_type=jnp.float32,
    ) / math.sqrt(HD)
    positions = jnp.arange(unit_len, dtype=jnp.int32)
    distance = positions[:, None] - positions[None, :]
    allowed = (doc_units[:, :, None] == doc_units[:, None, :]) & (
        (distance >= 0) & (distance < WIN)
    )[None]
    scores = jnp.where(allowed[:, None], scores, -1e30)
    row_max = jnp.max(scores, axis=3, keepdims=True)
    exp_scores = jnp.exp(scores - row_max)
    attn_probs = (exp_scores / jnp.sum(exp_scores, axis=3, keepdims=True)).astype(jnp.bfloat16)
    mixed_heads = jnp.einsum(
        "uhqk,ukhd->uqhd",
        attn_probs,
        value_units.reshape(head_shape),
        preferred_element_type=jnp.float32,
    )
    return (
        resid_units.astype(jnp.float32) + mixed_heads.reshape(unit_count, unit_len, columns)
    ).astype(jnp.bfloat16)


def pack_units(send_table, unit_data):
    return jnp.einsum(
        "tsu,uic->tsic", send_table, unit_data, preferred_element_type=jnp.float32
    ).astype(jnp.bfloat16)


def unpack_units(recv_table, arrived):
    return jnp.einsum(
        "jts,tsic->jic", recv_table, arrived, preferred_element_type=jnp.float32
    ).astype(jnp.bfloat16)


def exchange(block, distance):
    groups = lax.axis_size("dp")
    return lax.ppermute(block, "dp", [(i, i ^ distance) for i in range(groups)])


def first_hops(block):
    groups = lax.axis_size("dp")
    distances = (1, 2) if groups == 4 else range(1, groups)
    return [exchange(block, o) for o in distances]


def far_halves(arrived):
    if lax.axis_size("dp") != 4:
        return []
    half = arrived[0].shape[0] // 2
    return [arrived[0][:half], arrived[1][half:]]


def second_hops(halves):
    return [exchange(half, 2 - index) for index, half in enumerate(halves)]


def after(value, *earlier):
    return lax.optimization_barrier((value, *earlier))


def deal(block, share):
    groups = lax.axis_size("dp")
    me = lax.axis_index("dp")
    parts = []
    for o in range(groups):
        piece = lax.dynamic_slice_in_dim(block, (me ^ o) * share, share, 1)
        parts.append(piece if o == 0 else exchange(piece, o))
    return parts


def pick_gains(langs, norm_gains):
    gains = jnp.zeros((langs.shape[0], norm_gains.shape[1]), jnp.float32)
    for index in range(norm_gains.shape[0]):
        gains = jnp.where((langs == index)[:, None], norm_gains[index][None, :], gains)
    return gains


def over_tokens(left, right):
    return lax.dot_general(
        left, right, (((0,), (0,)), ((), ())), preferred_element_type=jnp.float32
    )


def times_transposed(left, weight):
    return lax.dot_general(
        left, weight, (((1,), (1,)), ((), ())), preferred_element_type=jnp.float32
    )


def scatter_rows(part):
    return lax.psum_scatter(
        part, "tensor", scatter_dimension=0, tiled=True
    ).astype(jnp.float32)


def per_device(
    query_states,
    key_states,
    value_states,
    residual,
    norm_gains,
    lang_labels,
    doc_lengths,
    destinations,
    gate_weight,
    up_weight,
    down_weight,
    out_cotangent,
):
    groups = lax.axis_size("dp")
    shards = lax.axis_size("tensor")
    my_group = lax.axis_index("dp")
    total_units = destinations.shape[0]
    per_group = total_units // groups
    columns = query_states.shape[1]
    width_d = gate_weight.shape[0]
    share = width_d // groups
    tok_group = per_group * UNIT
    rows_here = out_cotangent.shape[0]
    first_unit = my_group * per_group

    cot_full = lax.all_gather(out_cotangent, "tensor", axis=0, tiled=True)

    own_docs = doc_index(lax.dynamic_slice_in_dim(doc_lengths, first_unit, per_group), UNIT)
    unit_shape = (per_group, UNIT, columns)
    mixed_units = attend(
        query_states.reshape(unit_shape),
        key_states.reshape(unit_shape),
        value_states.reshape(unit_shape),
        residual.reshape(unit_shape),
        own_docs,
    )

    unit_index = jnp.arange(total_units, dtype=jnp.int32)
    source_group = unit_index // per_group
    earlier = unit_index[None, :] < unit_index[:, None]
    same_target = destinations[None, :] == destinations[:, None]
    same_source = source_group[None, :] == source_group[:, None]
    send_rank = jnp.sum((earlier & same_target & same_source).astype(jnp.int32), axis=1)
    arrival = jnp.sum((earlier & same_target).astype(jnp.int32), axis=1)
    own_targets = lax.dynamic_slice_in_dim(destinations, first_unit, per_group)
    own_ranks = lax.dynamic_slice_in_dim(send_rank, first_unit, per_group)
    group_ids = jnp.arange(groups, dtype=jnp.int32)
    slot_ids = jnp.arange(CAP, dtype=jnp.int32)
    send_table = (
        (own_targets[None, None, :] == group_ids[:, None, None])
        & (own_ranks[None, None, :] == slot_ids[None, :, None])
    ).astype(jnp.bfloat16)
    arrive_ids = jnp.arange(per_group, dtype=jnp.int32)
    landing = (destinations == my_group)[None, :] & (arrival[None, :] == arrive_ids[:, None])
    recv_table = jnp.sum(
        (
            landing[:, None, None, :]
            & (source_group[None, None, None, :] == group_ids[None, :, None, None])
            & (send_rank[None, None, None, :] == slot_ids[None, None, :, None])
        ).astype(jnp.int32),
        axis=3,
    ).astype(jnp.bfloat16)
    moved_langs = jnp.sum(landing.astype(jnp.int32) * lang_labels[None, :], axis=1)
    lang_tokens = jnp.broadcast_to(moved_langs[:, None], (per_group, UNIT)).reshape(tok_group)

    moved = lax.all_to_all(
        pack_units(send_table, mixed_units), "dp", split_axis=0, concat_axis=0, tiled=True
    )
    stream_cols = unpack_units(recv_table, moved).reshape(tok_group, columns)
    stream_cols, cot_full = after(stream_cols, cot_full)
    stream_full = lax.all_gather(stream_cols, "tensor", axis=1, tiled=True)

    grad_hidden = times_transposed(cot_full, down_weight)
    cot_parts = deal(cot_full, share)
    stream_full, grad_hidden, *cot_parts = after(stream_full, grad_hidden, *cot_parts)
    cot_all = jnp.concatenate(cot_parts, axis=0)

    stream_f = stream_full.astype(jnp.float32)
    scaled_full = (stream_f * pick_gains(lang_tokens, norm_gains)).astype(jnp.bfloat16)
    inv_rms = lax.rsqrt(jnp.sum(stream_f * stream_f, axis=1) / width_d + 1e-05)

    my_start = lax.axis_index("tensor") * rows_here
    stream_rows = lax.dynamic_slice_in_dim(stream_full, my_start, rows_here, 0).astype(jnp.float32)
    lang_rows = lax.dynamic_slice_in_dim(lang_tokens, my_start, rows_here)
    gain_rows = pick_gains(lang_rows, norm_gains)
    scaled_rows = (stream_rows * gain_rows).astype(jnp.bfloat16)
    rms_rows = lax.dynamic_slice_in_dim(inv_rms, my_start, rows_here, 0)

    gate_acc = jnp.dot(scaled_full, gate_weight, preferred_element_type=jnp.float32)
    up_acc = jnp.dot(scaled_full, up_weight, preferred_element_type=jnp.float32)
    act_gate = inv_rms[:, None] * gate_acc
    act_up = inv_rms[:, None] * up_acc
    sigma = jax.nn.sigmoid(act_gate)
    silu = act_gate * sigma
    hidden = (silu * act_up).astype(jnp.bfloat16)
    weighted = inv_rms[:, None] * grad_hidden
    grad_gate = (weighted * act_up * sigma * (1.0 + act_gate * (1.0 - sigma))).astype(jnp.bfloat16)
    grad_up = (weighted * silu).astype(jnp.bfloat16)

    hidden_near = first_hops(hidden)
    near_count = len(hidden_near)
    dealt = deal(scaled_rows, share)
    out_part = jnp.dot(hidden, down_weight, preferred_element_type=jnp.float32)
    out_part = out_part.astype(jnp.bfloat16)

    grad_gate, grad_up, out_part, *rest = after(grad_gate, grad_up, out_part, *hidden_near, *dealt)
    hidden_near, dealt = rest[:near_count], rest[near_count:]
    gathered = lax.all_gather(jnp.stack(dealt, axis=0), "tensor", axis=0)
    out_total = scatter_rows(out_part)
    gate_near = first_hops(grad_gate)
    hidden_far = second_hops(far_halves(hidden_near))
    far_count = len(hidden_far)
    back_part = times_transposed(grad_gate, gate_weight)
    back_part = (back_part + times_transposed(grad_up, up_weight)).astype(jnp.bfloat16)

    grad_up, back_part, *rest = after(grad_up, back_part, *gate_near, *hidden_far)
    gate_near, hidden_far = rest[:near_count], rest[near_count:]
    up_near = first_hops(grad_up)
    gate_far = second_hops(far_halves(gate_near))
    back_total = scatter_rows(back_part)
    hidden, gathered, out_total = after(hidden, gathered, out_total)
    down_grad = over_tokens(
        jnp.concatenate([hidden, *hidden_near, *hidden_far], axis=0), cot_all
    ).astype(jnp.bfloat16)

    down_grad, *rest = after(down_grad, *up_near, *gate_far)
    up_near, gate_far = rest[:near_count], rest[near_count:]
    up_far = second_hops(far_halves(up_near))
    scaled_all = gathered.transpose(1, 0, 2, 3).reshape(groups * tok_group, share)
    gate_grad = over_tokens(
        scaled_all, jnp.concatenate([grad_gate, *gate_near, *gate_far], axis=0)
    ).astype(jnp.bfloat16)
    up_grad = over_tokens(
        scaled_all, jnp.concatenate([grad_up, *up_near, *up_far], axis=0)
    ).astype(jnp.bfloat16)

    layer_out = (stream_rows + out_total).astype(jnp.bfloat16)
    dot_sum = jnp.sum(scaled_rows.astype(jnp.float32) * back_total, axis=1)
    input_grad = (
        out_cotangent.astype(jnp.float32)
        + gain_rows * back_total
        - (rms_rows * rms_rows / width_d)[:, None] * stream_rows * dot_sum[:, None]
    ).astype(jnp.bfloat16)
    return (layer_out, input_grad, gate_grad, up_grad, down_grad)


def solution(mesh):
    return jax.shard_map(
        per_device,
        mesh=mesh,
        in_specs=(
            P("dp", "tensor"),
            P("dp", "tensor"),
            P("dp", "tensor"),
            P("dp", "tensor"),
            P(),
            P(),
            P(),
            P(),
            P(None, "tensor"),
            P(None, "tensor"),
            P("tensor", None),
            P(("dp", "tensor"), None),
        ),
        out_specs=(
            P(("dp", "tensor"), None),
            P(("dp", "tensor"), None),
            P("dp", "tensor"),
            P("dp", "tensor"),
            P("tensor", "dp"),
        ),
        check_vma=False,
    )
```

profile of v0, /device:TPU:0, one launch (start us, length us, event | category | flops | bytes accessed | tf_op | source)
XLA Modules:
  0.0 296.4 jit_solution(9437879503212228150)
XLA Ops:
  15.7 5.2 %all-to-all-start = ((bf16[4,2,48,512]{3,1,2,0:T(2,128)(2,1)}), bf16[4,2,48,512]{3,1,2,0:T(2,128)(2,1)S(1)}, u32[]{:S(2)}, u32[]{:S(2)}) async-start(bf16[4,2,48,512]{3,1,2,0:T(2,128)(2,1)} %copy.57), calls=%async_computation | async-start | bytes 786432 | tf_op jit(solution)/shard_map/all_to_all | solution.py:188
  21.1 6.3 %all-to-all-done = bf16[4,2,48,512]{3,1,2,0:T(2,128)(2,1)S(1)} async-done(((bf16[4,2,48,512]{3,1,2,0:T(2,128)(2,1)}), bf16[4,2,48,512]{3,1,2,0:T(2,128)(2,1)S(1)}, u32[]{:S(2)}, u32[]{:S(2)}) %all-to-all-start) | async-done | bytes 393248 | tf_op jit(solution)/shard_map/all_to_all | solution.py:188
  29.0 21.7 %all-gather.5.cloned.1.call-done = bf16[384,4096]{1,0:T(8,128)(2,1)} async-done(((bf16[48,4096]{1,0:T(8,128)(2,1)}), bf16[384,4096]{1,0:T(8,128)(2,1)}) %all-gather.5.cloned.1.call-update) | async-done | bytes 3145744 | tf_op jit(solution)/shard_map/all_gather | solution.py:148
  51.3 3.4 %constant_dynamic-slice_fusion.4 = (bf16[384,1024]{1,0:T(8,128)(2,1)S(1)}, bf16[384,1024]{1,0:T(8,128)(2,1)S(1)}, bf16[384,1024]{1,0:T(8,128)(2,1)S(1)}, bf16[384,1024]{1,0:T(8,128)(2,1)}) fusion(bf16[384,4096]{1,0:T(8,128)(2,1)} %all-gather.5.cloned.1.call-done, s32[]{:T(128)S(6)} %select_n.81, s32[]{:T(128)S(6)} %select_n.80, s32[]{:T(128)S(6)} %select_n.79, ...), kind=kLoop, calls=%fused_computation.92 | loop fusion | bytes 6291472 | tf_op jit(solution)/shard_map/dynamic_slice | solution.py:92
  58.1 11.1 %fusion.49 = f32[384,1792]{1,0:T(8,128)} fusion(bf16[384,4096]{1,0:T(8,128)(2,1)S(1)} %copy-done.5, bf16[1792,4096]{1,0:T(8,128)(2,1)} %param.22), kind=kOutput, calls=%fused_computation.123 | convolution fusion | flops 5637144576 | bytes 20578304 | tf_op jit(solution)/shard_map/dot_general | solution.py:111
  69.3 5.7 %collective-permute-done = bf16[384,1024]{1,0:T(8,128)(2,1)S(1)} collective-permute-done((bf16[384,1024]{1,0:T(8,128)(2,1)S(1)}, bf16[384,1024]{1,0:T(8,128)(2,1)S(1)}, u32[]{:S(2)}, u32[]{:S(2)}) %collective-permute-start) | collective-permute-done | bytes 786464 | tf_op jit(solution)/shard_map/ppermute | solution.py:63
  75.0 17.5 %collective-permute-done.1 = bf16[384,1024]{1,0:T(8,128)(2,1)} collective-permute-done((bf16[384,1024]{1,0:T(8,128)(2,1)S(1)}, bf16[384,1024]{1,0:T(8,128)(2,1)}, u32[]{:S(2)}, u32[]{:S(2)}) %collective-permute-start.1) | collective-permute-done | bytes 786464 | tf_op jit(solution)/shard_map/ppermute | solution.py:63
  92.5 2.6 fusion.1
  95.1 14.2 %convolution_multiply_fusion.1 = f32[384,1792]{1,0:T(8,128)S(1)} fusion(bf16[4096,1792]{1,0:T(8,128)(2,1)} %param.20, f32[384]{0:T(512)S(1)} %add_rsqrt_fusion, bf16[384,4096]{1,0:T(8,128)(2,1)} %all-gather.7.cloned.1.call-done, f32[4096]{0:T(1024)S(1)} %bitcast.74, f32[4096]{0:T(1024)S(1)} %bitcast.79, f32[4096]{0:T(1024)S(1)} %bitcast.69, ...), kind=kOutput, calls=%fused_computation.18 | convolution fusion | flops 5648842752 | bytes 20646912 | tf_op jit(solution)/shard_map/dot_general | solution.py:211
  109.4 11.5 %convolution_multiply_fusion = f32[384,1792]{1,0:T(8,128)S(1)} fusion(bf16[4096,1792]{1,0:T(8,128)(2,1)} %param.21, f32[384]{0:T(512)S(1)} %add_rsqrt_fusion, bf16[384,4096]{1,0:T(8,128)(2,1)S(1)} %copy-done.2, f32[4096]{0:T(1024)S(1)} %bitcast.75, f32[4096]{0:T(1024)S(1)} %bitcast.80, f32[4096]{0:T(1024)S(1)} %bitcast.70, f32[4096]{0:T(1024)S(1)} %bitcast.65, ...), kind=kOutput, calls=%fused_computation.17 | convolution fusion | flops 5648842752 | bytes 20646912 | tf_op jit(solution)/shard_map/dot_general | solution.py:212
  120.9 3.2 %multiply_convert_fusion = (bf16[384,1792]{1,0:T(8,128)(2,1)}, bf16[384,1792]{1,0:T(8,128)(2,1)}, bf16[384,1792]{1,0:T(8,128)(2,1)}) fusion(f32[384,1792]{1,0:T(8,128)S(1)} %copy-done.7, f32[384]{0:T(512)S(1)} %add_rsqrt_fusion, f32[384,1792]{1,0:T(8,128)S(1)} %convolution_multiply_fusion.1, f32[384,1792]{1,0:T(8,128)S(1)} %convolution_multiply_fusion), kind=kLoop, calls=%fused_computation.19 | loop fusion | flops 11010048 | bytes 12387840 | tf_op jit(solution)/shard_map/convert_element_type | solution.py:220
  130.7 9.0 %convolution_convert_fusion = bf16[384,4096]{1,0:T(8,128)(2,1)} fusion(bf16[384,1792]{1,0:T(8,128)(2,1)} %get-tuple-element.54, bf16[1792,4096]{1,0:T(8,128)(2,1)S(1)} %bitcast.88), kind=kOutput, calls=%fused_computation.6 | convolution fusion | flops 5638717440 | bytes 19202048 | tf_op jit(solution)/shard_map/dot_general | solution.py:225
  139.7 19.1 %collective-permute-done.5 = bf16[48,1024]{1,0:T(8,128)(2,1)S(1)} collective-permute-done((bf16[48,1024]{1,0:T(8,128)(2,1)}, bf16[48,1024]{1,0:T(8,128)(2,1)S(1)}, u32[]{:S(2)}, u32[]{:S(2)}) %collective-permute-start.5) | collective-permute-done | bytes 98336 | tf_op jit(solution)/shard_map/ppermute | solution.py:63
  170.7 9.6 %fusion.50 = f32[384,4096]{1,0:T(8,128)S(1)} fusion(bf16[384,1792]{1,0:T(8,128)(2,1)} %get-tuple-element.61, bf16[4096,1792]{1,0:T(8,128)(2,1)} %param.21), kind=kOutput, calls=%fused_computation.124 | convolution fusion | flops 5637144576 | bytes 22347776 | tf_op jit(solution)/shard_map/dot_general | solution.py:111
  180.3 16.4 %add_convert_fusion = bf16[384,4096]{1,0:T(8,128)(2,1)} fusion(f32[384,4096]{1,0:T(8,128)S(1)} %fusion.50, bf16[384,1792]{1,0:T(8,128)(2,1)S(1)} %copy-done.4, bf16[4096,1792]{1,0:T(8,128)(2,1)} %param.20), kind=kOutput, calls=%fused_computation.5 | convolution fusion | flops 5640290304 | bytes 25493504 | tf_op jit(solution)/shard_map/dot_general | solution.py:111
  196.7 2.7 constant_dynamic-update-slice_fusion.9
  199.4 8.4 %collective-permute-done.10 = bf16[192,1792]{1,0:T(8,128)(2,1)} collective-permute-done((bf16[192,1792]{1,0:T(8,128)(2,1)}, bf16[192,1792]{1,0:T(8,128)(2,1)}, u32[]{:S(2)}, u32[]{:S(2)}) %collective-permute-start.10) | collective-permute-done | bytes 688160 | tf_op jit(solution)/shard_map/ppermute | solution.py:63
  215.9 2.6 constant_dynamic-update-slice_fusion.8
  218.5 3.1 %constant_dynamic-update-slice_fusion.7 = (bf16[1536,1792]{1,0:T(8,128)(2,1)}, bf16[1536,1792]{1,0:T(8,128)(2,1)}) fusion(bf16[1536,1792]{1,0:T(8,128)(2,1)} %constant_dynamic-update-slice_fusion.8, bf16[384,1792]{1,0:T(8,128)(2,1)} %collective-permute-done.9, bf16[384,1792]{1,0:T(8,128)(2,1)S(1)} %copy-done.3), kind=kLoop, calls=%fused_computation.63 | loop fusion | bytes 5505024
  223.7 15.3 %all-gather.9.cloned.1.call-done = bf16[32,48,1024]{2,1,0:T(8,128)(2,1)} async-done(((bf16[4,48,1024]{2,1,0:T(8,128)(2,1)}), bf16[32,48,1024]{2,1,0:T(8,128)(2,1)}) %all-gather.9.cloned.1.call-update) | async-done | bytes 3145744 | tf_op jit(solution)/shard_map/all_gather | solution.py:230
  245.7 9.0 %convolution_convert_fusion.3 = bf16[1792,1024]{1,0:T(8,128)(2,1)} fusion(bf16[1536,1792]{1,0:T(8,128)(2,1)S(1)} %constant_dynamic-update-slice_fusion, bf16[384,1024]{1,0:T(8,128)(2,1)} %collective-permute-done.2, bf16[384,1024]{1,0:T(8,128)(2,1)} %collective-permute-done.1, bf16[384,1024]{1,0:T(8,128)(2,1)S(1)} %copy-done.20, ...), kind=kOutput, calls=%fused_computation.9 | convolution fusion | flops 5651562496 | bytes 12320768 | tf_op jit(solution)/shard_map/dot_general | solution.py:105
  264.7 10.2 %convolution_convert_fusion.2 = bf16[1024,1792]{1,0:T(8,128)(2,1)} fusion(bf16[1536,1024]{1,0:T(8,128)(2,1)S(1)} %bitcast.57, bf16[1536,1792]{1,0:T(8,128)(2,1)} %constant_dynamic-update-slice_fusion.5), kind=kOutput, calls=%fused_computation.8 | convolution fusion | flops 5638979584 | bytes 12320768 | tf_op jit(solution)/shard_map/dot_general | solution.py:105
  278.0 7.7 %convolution_convert_fusion.1 = bf16[1024,1792]{1,0:T(8,128)(2,1)} fusion(bf16[1536,1024]{1,0:T(8,128)(2,1)S(1)} %bitcast.58, bf16[1536,1792]{1,0:T(8,128)(2,1)S(1)} %constant_dynamic-update-slice_fusion.10), kind=kOutput, calls=%fused_computation.7 | convolution fusion | flops 5638979584 | bytes 12320768 | tf_op jit(solution)/shard_map/dot_general | solution.py:105
  287.2 2.7 fusion.17
  (160 shorter events, 63.9 us)
Async XLA Ops:
  7.2 43.5 %all-gather.5.cloned.1.call-start = ((), (), s32[]{:S(2)}) async-start(), calls=%async_computation.3 | async-start | bytes 3538944 | tf_op jit(solution)/shard_map/all_gather | solution.py:148
  15.7 11.8 %all-to-all-start = ((bf16[4,2,48,512]{3,1,2,0:T(2,128)(2,1)}), bf16[4,2,48,512]{3,1,2,0:T(2,128)(2,1)S(1)}, u32[]{:S(2)}, u32[]{:S(2)}) async-start(bf16[4,2,48,512]{3,1,2,0:T(2,128)(2,1)} %copy.57), calls=%async_computation | async-start | bytes 786432 | tf_op jit(solution)/shard_map/all_to_all | solution.py:188
  20.8 71.6 %all-gather.7.cloned.1.call-start = ((), (), s32[]{:S(2)}) async-start(), calls=%async_computation.4 | async-start | bytes 3538944 | tf_op jit(solution)/shard_map/all_gather | solution.py:193
  50.7 170.9 %reduce-scatter.3.cloned.1.call-start = ((), (), s32[]{:S(2)}) async-start(), calls=%async_computation.5 | async-start | bytes 3538944 | tf_op jit(solution)/shard_map/reduce_scatter | solution.py:117
  54.6 20.4 %collective-permute-start = (bf16[384,1024]{1,0:T(8,128)(2,1)S(1)}, bf16[384,1024]{1,0:T(8,128)(2,1)S(1)}, u32[]{:S(2)}, u32[]{:S(2)}) collective-permute-start(bf16[384,1024]{1,0:T(8,128)(2,1)S(1)} %get-tuple-element.78), channel_id=1, source_target_pairs={{0,8},{8,0},{16,24},{24,16},{1,9},{9,1},{17,25},{25,17},{2,10},{10... | collective-permute-start | bytes 2359304 | tf_op jit(solution)/shard_map/ppermute | solution.py:63
  56.1 36.4 %collective-permute-start.1 = (bf16[384,1024]{1,0:T(8,128)(2,1)S(1)}, bf16[384,1024]{1,0:T(8,128)(2,1)}, u32[]{:S(2)}, u32[]{:S(2)}) collective-permute-start(bf16[384,1024]{1,0:T(8,128)(2,1)S(1)} %get-tuple-element.77), channel_id=1, source_target_pairs={{0,16},{8,24},{16,0},{24,8},{1,17},{9,25},{17,1},{25,9},{2,18},{10... | collective-permute-start | bytes 2359304 | tf_op jit(solution)/shard_map/ppermute | solution.py:63
  57.6 34.9 %collective-permute-start.2 = (bf16[384,1024]{1,0:T(8,128)(2,1)S(1)}, bf16[384,1024]{1,0:T(8,128)(2,1)}, u32[]{:S(2)}, u32[]{:S(2)}) collective-permute-start(bf16[384,1024]{1,0:T(8,128)(2,1)S(1)} %get-tuple-element.76), channel_id=1, source_target_pairs={{0,24},{8,16},{16,8},{24,0},{1,25},{9,17},{17,9},{25,1},{2,26},{10... | collective-permute-start | bytes 2359304 | tf_op jit(solution)/shard_map/ppermute | solution.py:63
  124.2 36.8 %collective-permute-start.3 = (bf16[384,1792]{1,0:T(8,128)(2,1)}, bf16[384,1792]{1,0:T(8,128)(2,1)}, u32[]{:S(2)}, u32[]{:S(2)}) collective-permute-start(bf16[384,1792]{1,0:T(8,128)(2,1)} %get-tuple-element.54), channel_id=1, source_target_pairs={{0,8},{8,0},{16,24},{24,16},{1,9},{9,1},{17,25},{25,17},{2,10},{10... | collective-permute-start | bytes 4128776 | tf_op jit(solution)/shard_map/ppermute | solution.py:63
  125.3 35.7 %collective-permute-start.4 = (bf16[384,1792]{1,0:T(8,128)(2,1)}, bf16[384,1792]{1,0:T(8,128)(2,1)}, u32[]{:S(2)}, u32[]{:S(2)}) collective-permute-start(bf16[384,1792]{1,0:T(8,128)(2,1)} %get-tuple-element.54), channel_id=1, source_target_pairs={{0,16},{8,24},{16,0},{24,8},{1,17},{9,25},{17,1},{25,9},{2,18},{10... | collective-permute-start | bytes 4128776 | tf_op jit(solution)/shard_map/ppermute | solution.py:63
  127.2 31.6 %collective-permute-start.5 = (bf16[48,1024]{1,0:T(8,128)(2,1)}, bf16[48,1024]{1,0:T(8,128)(2,1)S(1)}, u32[]{:S(2)}, u32[]{:S(2)}) collective-permute-start(bf16[48,1024]{1,0:T(8,128)(2,1)} %get-tuple-element.82), channel_id=1, source_target_pairs={{0,8},{8,0},{16,24},{24,16},{1,9},{9,1},{17,25},{25,17},{2,10},{10... | collective-permute-start | bytes 294920 | tf_op jit(solution)/shard_map/ppermute | solution.py:63
  128.7 32.3 %collective-permute-start.6 = (bf16[48,1024]{1,0:T(8,128)(2,1)}, bf16[48,1024]{1,0:T(8,128)(2,1)S(1)}, u32[]{:S(2)}, u32[]{:S(2)}) collective-permute-start(bf16[48,1024]{1,0:T(8,128)(2,1)} %get-tuple-element.81), channel_id=1, source_target_pairs={{0,16},{8,24},{16,0},{24,8},{1,17},{9,25},{17,1},{25,9},{2,18},{10... | collective-permute-start | bytes 294920 | tf_op jit(solution)/shard_map/ppermute | solution.py:63
  129.2 31.7 %collective-permute-start.7 = (bf16[48,1024]{1,0:T(8,128)(2,1)}, bf16[48,1024]{1,0:T(8,128)(2,1)S(1)}, u32[]{:S(2)}, u32[]{:S(2)}) collective-permute-start(bf16[48,1024]{1,0:T(8,128)(2,1)} %get-tuple-element.80), channel_id=1, source_target_pairs={{0,24},{8,16},{16,8},{24,0},{1,25},{9,17},{17,9},{25,1},{2,26},{10... | collective-permute-start | bytes 294920 | tf_op jit(solution)/shard_map/ppermute | solution.py:63
  161.0 77.9 %all-gather.9.cloned.1.call-start = ((), (), s32[]{:S(2)}) async-start(), calls=%async_computation.7 | async-start | bytes 3538944 | tf_op jit(solution)/shard_map/all_gather | solution.py:230
  161.9 123.8 %reduce-scatter.5.cloned.1.call-start = ((), (), s32[]{:S(2)}) async-start(), calls=%async_computation.6 | async-start | bytes 3538944 | tf_op jit(solution)/shard_map/reduce_scatter | solution.py:117
  162.6 45.1 %collective-permute-start.8 = (bf16[384,1792]{1,0:T(8,128)(2,1)}, bf16[384,1792]{1,0:T(8,128)(2,1)}, u32[]{:S(2)}, u32[]{:S(2)}) collective-permute-start(bf16[384,1792]{1,0:T(8,128)(2,1)} %get-tuple-element.47), channel_id=1, source_target_pairs={{0,8},{8,0},{16,24},{24,16},{1,9},{9,1},{17,25},{25,17},{2,10},{10... | collective-permute-start | bytes 4128776 | tf_op jit(solution)/shard_map/ppermute | solution.py:63
  163.2 44.5 %collective-permute-start.9 = (bf16[384,1792]{1,0:T(8,128)(2,1)}, bf16[384,1792]{1,0:T(8,128)(2,1)}, u32[]{:S(2)}, u32[]{:S(2)}) collective-permute-start(bf16[384,1792]{1,0:T(8,128)(2,1)} %get-tuple-element.47), channel_id=1, source_target_pairs={{0,16},{8,24},{16,0},{24,8},{1,17},{9,25},{17,1},{25,9},{2,18},{10... | collective-permute-start | bytes 4128776 | tf_op jit(solution)/shard_map/ppermute | solution.py:63
  166.7 41.1 %collective-permute-start.10 = (bf16[192,1792]{1,0:T(8,128)(2,1)}, bf16[192,1792]{1,0:T(8,128)(2,1)}, u32[]{:S(2)}, u32[]{:S(2)}) collective-permute-start(bf16[192,1792]{1,0:T(8,128)(2,1)} %slice.38), channel_id=1, source_target_pairs={{0,16},{8,24},{16,0},{24,8},{1,17},{9,25},{17,1},{25,9},{2,18},{10... | collective-permute-start | bytes 2064392 | tf_op jit(solution)/shard_map/ppermute | solution.py:63
  169.2 38.5 %collective-permute-start.11 = (bf16[192,1792]{1,0:T(8,128)(2,1)}, bf16[192,1792]{1,0:T(8,128)(2,1)}, u32[]{:S(2)}, u32[]{:S(2)}) collective-permute-start(bf16[192,1792]{1,0:T(8,128)(2,1)} %slice.39), channel_id=1, source_target_pairs={{0,8},{8,0},{16,24},{24,16},{1,9},{9,1},{17,25},{25,17},{2,10},{10... | collective-permute-start | bytes 2064392 | tf_op jit(solution)/shard_map/ppermute | solution.py:63
  207.7 47.3 %collective-permute-start.12 = (bf16[384,1792]{1,0:T(8,128)(2,1)}, bf16[384,1792]{1,0:T(8,128)(2,1)}, u32[]{:S(2)}, u32[]{:S(2)}) collective-permute-start(bf16[384,1792]{1,0:T(8,128)(2,1)} %get-tuple-element.61), channel_id=1, source_target_pairs={{0,8},{8,0},{16,24},{24,16},{1,9},{9,1},{17,25},{25,17},{2,10},{10... | collective-permute-start | bytes 4128776 | tf_op jit(solution)/shard_map/ppermute | solution.py:63
  209.2 45.9 %collective-permute-start.13 = (bf16[384,1792]{1,0:T(8,128)(2,1)}, bf16[384,1792]{1,0:T(8,128)(2,1)}, u32[]{:S(2)}, u32[]{:S(2)}) collective-permute-start(bf16[384,1792]{1,0:T(8,128)(2,1)} %get-tuple-element.61), channel_id=1, source_target_pairs={{0,16},{8,24},{16,0},{24,8},{1,17},{9,25},{17,1},{25,9},{2,18},{10... | collective-permute-start | bytes 4128776 | tf_op jit(solution)/shard_map/ppermute | solution.py:63
  211.8 43.2 %collective-permute-start.14 = (bf16[192,1792]{1,0:T(8,128)(2,1)}, bf16[192,1792]{1,0:T(8,128)(2,1)}, u32[]{:S(2)}, u32[]{:S(2)}) collective-permute-start(bf16[192,1792]{1,0:T(8,128)(2,1)} %slice.40), channel_id=1, source_target_pairs={{0,16},{8,24},{16,0},{24,8},{1,17},{9,25},{17,1},{25,9},{2,18},{10... | collective-permute-start | bytes 2064392 | tf_op jit(solution)/shard_map/ppermute | solution.py:63
  215.2 39.9 %collective-permute-start.15 = (bf16[192,1792]{1,0:T(8,128)(2,1)}, bf16[192,1792]{1,0:T(8,128)(2,1)}, u32[]{:S(2)}, u32[]{:S(2)}) collective-permute-start(bf16[192,1792]{1,0:T(8,128)(2,1)} %slice.41), channel_id=1, source_target_pairs={{0,8},{8,0},{16,24},{24,16},{1,9},{9,1},{17,25},{25,17},{2,10},{10... | collective-permute-start | bytes 2064392 | tf_op jit(solution)/shard_map/ppermute | solution.py:63
  256.2 21.6 %collective-permute-start.16 = (bf16[192,1792]{1,0:T(8,128)(2,1)S(1)}, bf16[192,1792]{1,0:T(8,128)(2,1)S(1)}, u32[]{:S(2)}, u32[]{:S(2)}) collective-permute-start(bf16[192,1792]{1,0:T(8,128)(2,1)S(1)} %slice.42), channel_id=1, source_target_pairs={{0,16},{8,24},{16,0},{24,8},{1,17},{9,25},{17,1},{25,9},{2,18},{10... | collective-permute-start | bytes 2064392 | tf_op jit(solution)/shard_map/ppermute | solution.py:63
  259.0 18.9 %collective-permute-start.17 = (bf16[192,1792]{1,0:T(8,128)(2,1)S(1)}, bf16[192,1792]{1,0:T(8,128)(2,1)S(1)}, u32[]{:S(2)}, u32[]{:S(2)}) collective-permute-start(bf16[192,1792]{1,0:T(8,128)(2,1)S(1)} %slice.43), channel_id=1, source_target_pairs={{0,8},{8,0},{16,24},{24,16},{1,9},{9,1},{17,25},{25,17},{2,10},{10... | collective-permute-start | bytes 2064392 | tf_op jit(solution)/shard_map/ppermute | solution.py:63
  (27 other events, 734.8 us)
Sparse Core Ops, SparseCore 0:
  9.7 40.9 all-gather.4
  52.9 37.1 all-gather.6
  161.2 38.2 reduce-scatter.2
  201.5 37.3 all-gather.8
  241.1 39.1 reduce-scatter.4
where the time goes:
time: 298 us; the launch traced here: 296 us
  matrix products  101 us (34%)
  waiting for transfers between devices  96.9 us (33%)
  local copies, waits for them, and re-layouts  43.4 us (15%)
  starting transfers between devices  25.6 us (9%)
  other arithmetic  15.5 us (5%)
  between operations  14.3 us (5%)
    ppermute x18, waiting for transfers between devices, exchange(): return lax.ppermute(block, 'dp', [(i, i ^ distance) for i in range(groups)])  52.8 us
    dot_general x3, matrix products, times_transposed(): lax.dot_general(left, weight, (((1,), (1,)), ((), ())), preferred_element...  37.2 us
    dot_general x3, matrix products, over_tokens(): lax.dot_general(left, right, (((0,), (0,)), ((), ())), preferred_element_...  27 us
    all_gather x1, waiting for transfers between devices, per_device(): cot_full = lax.all_gather(out_cotangent, 'tensor', axis=0, tiled=True)  21.7 us
    ppermute x18, starting transfers between devices, exchange(): return lax.ppermute(block, 'dp', [(i, i ^ distance) for i in range(groups)])  20.3 us
    unnamed x65, local copies, waits for them, and re-layouts  19 us
    all_gather x1, waiting for transfers between devices, per_device(): gathered = lax.all_gather(jnp.stack(dealt, axis=0), 'tensor', axis=0)  15.3 us
    dot_general x1, matrix products, per_device(): jnp.dot(scaled_full, gate_weight, preferred_element_type=jnp.float32)  14.2 us
  transfers between devices with their start and end apart: 24, of which 8 were waited for; matrix products, arithmetic and copies ran while one was open for 42% of the time, Pallas kernels for 0%

commit v1 on v0

--- a/solution.py
+++ b/solution.py
@@ -209,7 +209,9 @@
     rms_rows = lax.dynamic_slice_in_dim(inv_rms, my_start, rows_here, 0)
 
     gate_acc = jnp.dot(scaled_full, gate_weight, preferred_element_type=jnp.float32)
-    up_acc = jnp.dot(scaled_full, up_weight, preferred_element_type=jnp.float32)
+    scaled_up, *dealt = after(scaled_full, *deal(scaled_rows, share))
+    gathered = lax.all_gather(jnp.stack(dealt, axis=0), "tensor", axis=0)
+    up_acc = jnp.dot(scaled_up, up_weight, preferred_element_type=jnp.float32)
     act_gate = inv_rms[:, None] * gate_acc
     act_up = inv_rms[:, None] * up_acc
     sigma = jax.nn.sigmoid(act_gate)
@@ -221,37 +223,35 @@
 
     hidden_near = first_hops(hidden)
     near_count = len(hidden_near)
-    dealt = deal(scaled_rows, share)
     out_part = jnp.dot(hidden, down_weight, preferred_element_type=jnp.float32)
     out_part = out_part.astype(jnp.bfloat16)
 
-    grad_gate, grad_up, out_part, *rest = after(grad_gate, grad_up, out_part, *hidden_near, *dealt)
-    hidden_near, dealt = rest[:near_count], rest[near_count:]
-    gathered = lax.all_gather(jnp.stack(dealt, axis=0), "tensor", axis=0)
-    out_total = scatter_rows(out_part)
+    grad_gate, grad_up, out_part, *hidden_near = after(grad_gate, grad_up, out_part, *hidden_near)
     gate_near = first_hops(grad_gate)
     hidden_far = second_hops(far_halves(hidden_near))
-    far_count = len(hidden_far)
+    out_part, gathered = after(out_part, gathered)
+    out_total = scatter_rows(out_part)
     back_part = times_transposed(grad_gate, gate_weight)
     back_part = (back_part + times_transposed(grad_up, up_weight)).astype(jnp.bfloat16)
 
-    grad_up, back_part, *rest = after(grad_up, back_part, *gate_near, *hidden_far)
+    hidden, grad_up, back_part, *rest = after(hidden, grad_up, back_part, *gate_near, *hidden_far)
     gate_near, hidden_far = rest[:near_count], rest[near_count:]
-    up_near = first_hops(grad_up)
     gate_far = second_hops(far_halves(gate_near))
     back_total = scatter_rows(back_part)
-    hidden, gathered, out_total = after(hidden, gathered, out_total)
     down_grad = over_tokens(
         jnp.concatenate([hidden, *hidden_near, *hidden_far], axis=0), cot_all
     ).astype(jnp.bfloat16)
 
-    down_grad, *rest = after(down_grad, *up_near, *gate_far)
-    up_near, gate_far = rest[:near_count], rest[near_count:]
-    up_far = second_hops(far_halves(up_near))
+    grad_up, down_grad, out_total, *gate_far = after(grad_up, down_grad, out_total, *gate_far)
+    up_near = first_hops(grad_up)
     scaled_all = gathered.transpose(1, 0, 2, 3).reshape(groups * tok_group, share)
     gate_grad = over_tokens(
         scaled_all, jnp.concatenate([grad_gate, *gate_near, *gate_far], axis=0)
     ).astype(jnp.bfloat16)
+
+    gate_grad, *up_near = after(gate_grad, *up_near)
+    up_far = second_hops(far_halves(up_near))
+    scaled_rows, *up_far = after(scaled_rows, *up_far)
     up_grad = over_tokens(
         scaled_all, jnp.concatenate([grad_up, *up_near, *up_far], axis=0)
     ).astype(jnp.bfloat16)

time: 298 us -> 303 us (1.017)
  waiting for transfers between devices: 96.9 us -> 112 us
  matrix products: 101 us -> 92.9 us
    ppermute x18, waiting for transfers between devices: 52.8 us -> 82.9 us  [exchange(): return lax.ppermute(block, 'dp', [(i, i ^ distance) for i in range(groups)])]
    all_gather x1, waiting for transfers between devices: 15.3 us -> 0.01 us  [per_device(): gathered = lax.all_gather(jnp.stack(dealt, axis=0), 'tensor', axis=0)]
    dot_general x1, matrix products: 14.2 us -> 9.57 us  [per_device(): jnp.dot(scaled_full, gate_weight, preferred_element_type=jnp.float32)]
    unnamed x65 -> x69, local copies, waits for them, and re-layouts: 19 us -> 17.8 us
  transfers between devices with their start and end apart: 24 -> 24, of which waited for: 8 -> 11; matrix products, arithmetic and copies ran while one was open for 42% -> 47% of each run, Pallas kernels for 0% -> 0%
where the time goes in v1:
time: 303 us; the launch traced here: 302 us
  waiting for transfers between devices  112 us (37%)
  matrix products  92.9 us (31%)
  local copies, waits for them, and re-layouts  41.4 us (14%)
  starting transfers between devices  25.4 us (8%)
  other arithmetic  16.7 us (6%)
  between operations  14.4 us (5%)
    ppermute x18, waiting for transfers between devices, exchange(): return lax.ppermute(block, 'dp', [(i, i ^ distance) for i in range(groups)])  82.9 us
    dot_general x3, matrix products, times_transposed(): lax.dot_general(left, weight, (((1,), (1,)), ((), ())), preferred_element...  36.7 us
    dot_general x3, matrix products, over_tokens(): lax.dot_general(left, right, (((0,), (0,)), ((), ())), preferred_element_...  27.8 us
    all_gather x1, waiting for transfers between devices, per_device(): cot_full = lax.all_gather(out_cotangent, 'tensor', axis=0, tiled=True)  21.6 us
    ppermute x18, starting transfers between devices, exchange(): return lax.ppermute(block, 'dp', [(i, i ^ distance) for i in range(groups)])  19.9 us
    unnamed x69, local copies, waits for them, and re-layouts  17.8 us
    dot_general x1, matrix products, per_device(): up_acc = jnp.dot(scaled_up, up_weight, preferred_element_type=jnp.float32)  9.6 us
    dot_general x1, matrix products, per_device(): jnp.dot(scaled_full, gate_weight, preferred_element_type=jnp.float32)  9.57 us
  transfers between devices with their start and end apart: 24, of which 11 were waited for; matrix products, arithmetic and copies ran while one was open for 47% of the time, Pallas kernels for 0%

profile of v1, /device:TPU:0, one launch (start us, length us, event | category | flops | bytes accessed | tf_op | source)
XLA Modules:
  0.0 302.4 jit_solution(15601389975774624207)
XLA Ops:
  15.7 5.2 %all-to-all-start = ((bf16[4,2,48,512]{3,1,2,0:T(2,128)(2,1)}), bf16[4,2,48,512]{3,1,2,0:T(2,128)(2,1)S(1)}, u32[]{:S(2)}, u32[]{:S(2)}) async-start(bf16[4,2,48,512]{3,1,2,0:T(2,128)(2,1)} %copy.57), calls=%async_computation | async-start | bytes 786432 | tf_op jit(solution)/shard_map/all_to_all | solution.py:188
  21.2 6.3 %all-to-all-done = bf16[4,2,48,512]{3,1,2,0:T(2,128)(2,1)S(1)} async-done(((bf16[4,2,48,512]{3,1,2,0:T(2,128)(2,1)}), bf16[4,2,48,512]{3,1,2,0:T(2,128)(2,1)S(1)}, u32[]{:S(2)}, u32[]{:S(2)}) %all-to-all-start) | async-done | bytes 393248 | tf_op jit(solution)/shard_map/all_to_all | solution.py:188
  29.0 21.6 %all-gather.5.cloned.1.call-done = bf16[384,4096]{1,0:T(8,128)(2,1)} async-done(((bf16[48,4096]{1,0:T(8,128)(2,1)}), bf16[384,4096]{1,0:T(8,128)(2,1)}) %all-gather.5.cloned.1.call-update) | async-done | bytes 3145744 | tf_op jit(solution)/shard_map/all_gather | solution.py:148
  51.8 3.1 %constant_dynamic-slice_fusion.4 = (bf16[384,1024]{1,0:T(8,128)(2,1)S(1)}, bf16[384,1024]{1,0:T(8,128)(2,1)S(1)}, bf16[384,1024]{1,0:T(8,128)(2,1)S(1)}, bf16[384,1024]{1,0:T(8,128)(2,1)}) fusion(bf16[384,4096]{1,0:T(8,128)(2,1)} %all-gather.5.cloned.1.call-done, s32[]{:T(128)S(6)} %select_n.81, s32[]{:T(128)S(6)} %select_n.80, s32[]{:T(128)S(6)} %select_n.79, ...), kind=kLoop, calls=%fused_computation.92 | loop fusion | bytes 6291472 | tf_op jit(solution)/shard_map/dynamic_slice | solution.py:92
  58.4 11.1 %fusion.47 = f32[384,1792]{1,0:T(8,128)} fusion(bf16[384,4096]{1,0:T(8,128)(2,1)S(1)} %copy-done.3, bf16[1792,4096]{1,0:T(8,128)(2,1)} %param.22), kind=kOutput, calls=%fused_computation.123 | convolution fusion | flops 5637144576 | bytes 20578304 | tf_op jit(solution)/shard_map/dot_general | solution.py:111
  69.5 6.7 %collective-permute-done.2 = bf16[384,1024]{1,0:T(8,128)(2,1)S(1)} collective-permute-done((bf16[384,1024]{1,0:T(8,128)(2,1)S(1)}, bf16[384,1024]{1,0:T(8,128)(2,1)S(1)}, u32[]{:S(2)}, u32[]{:S(2)}) %collective-permute-start.2) | collective-permute-done | bytes 786464 | tf_op jit(solution)/shard_map/ppermute | solution.py:63
  76.2 16.2 %collective-permute-done.1 = bf16[384,1024]{1,0:T(8,128)(2,1)} collective-permute-done((bf16[384,1024]{1,0:T(8,128)(2,1)S(1)}, bf16[384,1024]{1,0:T(8,128)(2,1)}, u32[]{:S(2)}, u32[]{:S(2)}) %collective-permute-start.1) | collective-permute-done | bytes 786464 | tf_op jit(solution)/shard_map/ppermute | solution.py:63
  97.4 4.4 %fusion.1 = (f32[384]{0:T(512)S(1)}, bf16[384,4096]{1,0:T(8,128)(2,1)S(1)}) fusion(bf16[384,4096]{1,0:T(8,128)(2,1)} %all-gather.7.cloned.1.call-done, f32[4096]{0:T(1024)} %bitcast.71, pred[384]{0:T(512)(128)(4,1)} %get-tuple-element.105, f32[4096]{0:T(1024)} %bitcast.74, pred[384]{0:T(512)(128)(4,1)} %get-tuple-element.106, f32[4096]{0:T(1024)} %bitcast.68, ...), kind=kLoop, calls=%fused_computation.3 | loop fusion | flops 14155392 | bytes 6360064 | tf_op jit(solution)/shard_map/reduce_sum | solution.py:202
  103.0 9.6 %convolution_multiply_fusion.1 = f32[384,1792]{1,0:T(8,128)S(1)} fusion(bf16[384,4096]{1,0:T(8,128)(2,1)S(1)} %get-tuple-element.46, bf16[4096,1792]{1,0:T(8,128)(2,1)} %param.20, f32[384]{0:T(512)S(1)} %add_rsqrt_fusion), kind=kOutput, calls=%fused_computation.18 | convolution fusion | flops 5637832704 | bytes 20579840 | tf_op jit(solution)/shard_map/dot_general | solution.py:211
  112.6 9.6 %convolution_multiply_fusion = f32[384,1792]{1,0:T(8,128)S(1)} fusion(bf16[384,4096]{1,0:T(8,128)(2,1)S(1)} %get-tuple-element.46, bf16[4096,1792]{1,0:T(8,128)(2,1)} %param.21, f32[384]{0:T(512)S(1)} %add_rsqrt_fusion), kind=kOutput, calls=%fused_computation.17 | convolution fusion | flops 5637832704 | bytes 20579840 | tf_op jit(solution)/shard_map/dot_general | solution.py:214
  122.2 2.8 multiply_convert_fusion
  127.3 7.4 %convolution_convert_fusion = bf16[384,4096]{1,0:T(8,128)(2,1)} fusion(bf16[384,1792]{1,0:T(8,128)(2,1)S(1)} %get-tuple-element.53, bf16[1792,4096]{1,0:T(8,128)(2,1)S(1)} %bitcast.80), kind=kOutput, calls=%fused_computation.6 | convolution fusion | flops 5638717440 | bytes 19202048 | tf_op jit(solution)/shard_map/dot_general | solution.py:226
  134.8 22.0 %collective-permute-done.7 = bf16[384,1792]{1,0:T(8,128)(2,1)} collective-permute-done((bf16[384,1792]{1,0:T(8,128)(2,1)S(1)}, bf16[384,1792]{1,0:T(8,128)(2,1)}, u32[]{:S(2)}, u32[]{:S(2)}) %collective-permute-start.7) | collective-permute-done | bytes 1376288 | tf_op jit(solution)/shard_map/ppermute | solution.py:63
  166.4 9.3 %fusion.48 = f32[384,4096]{1,0:T(8,128)S(1)} fusion(bf16[384,1792]{1,0:T(8,128)(2,1)S(1)} %get-tuple-element.73, bf16[4096,1792]{1,0:T(8,128)(2,1)} %param.21), kind=kOutput, calls=%fused_computation.124 | convolution fusion | flops 5637144576 | bytes 22347776 | tf_op jit(solution)/shard_map/dot_general | solution.py:111
  175.7 16.4 %add_convert_fusion = bf16[384,4096]{1,0:T(8,128)(2,1)} fusion(f32[384,4096]{1,0:T(8,128)S(1)} %fusion.48, bf16[384,1792]{1,0:T(8,128)(2,1)S(1)} %copy-done.2, bf16[4096,1792]{1,0:T(8,128)(2,1)} %param.20), kind=kOutput, calls=%fused_computation.5 | convolution fusion | flops 5640290304 | bytes 25493504 | tf_op jit(solution)/shard_map/dot_general | solution.py:111
  193.5 10.9 %collective-permute-done.11 = bf16[192,1792]{1,0:T(8,128)(2,1)} collective-permute-done((bf16[192,1792]{1,0:T(8,128)(2,1)}, bf16[192,1792]{1,0:T(8,128)(2,1)}, u32[]{:S(2)}, u32[]{:S(2)}) %collective-permute-start.11) | collective-permute-done | bytes 688160 | tf_op jit(solution)/shard_map/ppermute | solution.py:63
  211.7 2.8 constant_dynamic-update-slice_fusion.4
  217.0 2.6 constant_dynamic-update-slice_fusion.3
  219.6 2.6 constant_dynamic-update-slice_fusion.2
  226.2 10.0 %convolution_convert_fusion.3 = bf16[1792,1024]{1,0:T(8,128)(2,1)} fusion(bf16[1536,1792]{1,0:T(8,128)(2,1)} %constant_dynamic-update-slice_fusion, bf16[384,1024]{1,0:T(8,128)(2,1)} %copy-done.24, bf16[384,1024]{1,0:T(8,128)(2,1)} %collective-permute-done.1, bf16[384,1024]{1,0:T(8,128)(2,1)} %collective-permute-done, bf16[384,1024]{1,0:T(8,128)(2,1)S(1)} %copy-done.8), kind=kOutput, calls=%fused_computation.9 | convolution fusion | flops 5651562496 | bytes 12320768 | tf_op jit(solution)/shard_map/dot_general | solution.py:105
  246.0 10.1 %convolution_convert_fusion.2 = bf16[1024,1792]{1,0:T(8,128)(2,1)} fusion(bf16[1536,1024]{1,0:T(8,128)(2,1)S(1)} %bitcast.59, bf16[1536,1792]{1,0:T(8,128)(2,1)} %constant_dynamic-update-slice_fusion.5), kind=kOutput, calls=%fused_computation.8 | convolution fusion | flops 5638979584 | bytes 12320768 | tf_op jit(solution)/shard_map/dot_general | solution.py:105
  256.1 12.7 %collective-permute-done.15 = bf16[384,1792]{1,0:T(8,128)(2,1)S(1)} collective-permute-done((bf16[384,1792]{1,0:T(8,128)(2,1)S(1)}, bf16[384,1792]{1,0:T(8,128)(2,1)S(1)}, u32[]{:S(2)}, u32[]{:S(2)}) %collective-permute-start.15) | collective-permute-done | bytes 1376288 | tf_op jit(solution)/shard_map/ppermute | solution.py:63
  273.7 10.5 %collective-permute-done.17 = bf16[192,1792]{1,0:T(8,128)(2,1)S(1)} collective-permute-done((bf16[192,1792]{1,0:T(8,128)(2,1)S(1)}, bf16[192,1792]{1,0:T(8,128)(2,1)S(1)}, u32[]{:S(2)}, u32[]{:S(2)}) %collective-permute-start.17) | collective-permute-done | bytes 688160 | tf_op jit(solution)/shard_map/ppermute | solution.py:63
  284.4 7.7 %convolution_convert_fusion.1 = bf16[1024,1792]{1,0:T(8,128)(2,1)} fusion(bf16[1536,1024]{1,0:T(8,128)(2,1)S(1)} %bitcast.60, bf16[1536,1792]{1,0:T(8,128)(2,1)S(1)} %constant_dynamic-update-slice_fusion.10), kind=kOutput, calls=%fused_computation.7 | convolution fusion | flops 5638979584 | bytes 12320768 | tf_op jit(solution)/shard_map/dot_general | solution.py:105
  (163 shorter events, 66.5 us)
Async XLA Ops:
  7.2 43.5 %all-gather.5.cloned.1.call-start = ((), (), s32[]{:S(2)}) async-start(), calls=%async_computation.3 | async-start | bytes 3538944 | tf_op jit(solution)/shard_map/all_gather | solution.py:148
  15.7 11.8 %all-to-all-start = ((bf16[4,2,48,512]{3,1,2,0:T(2,128)(2,1)}), bf16[4,2,48,512]{3,1,2,0:T(2,128)(2,1)S(1)}, u32[]{:S(2)}, u32[]{:S(2)}) async-start(bf16[4,2,48,512]{3,1,2,0:T(2,128)(2,1)} %copy.57), calls=%async_computation | async-start | bytes 786432 | tf_op jit(solution)/shard_map/all_to_all | solution.py:188
  20.9 71.6 %all-gather.7.cloned.1.call-start = ((), (), s32[]{:S(2)}) async-start(), calls=%async_computation.4 | async-start | bytes 3538944 | tf_op jit(solution)/shard_map/all_gather | solution.py:193
  50.7 107.4 %all-gather.9.cloned.1.call-start = ((), (), s32[]{:S(2)}) async-start(), calls=%async_computation.7 | async-start | bytes 3538944 | tf_op jit(solution)/shard_map/all_gather | solution.py:213
  54.9 21.3 %collective-permute-start.2 = (bf16[384,1024]{1,0:T(8,128)(2,1)S(1)}, bf16[384,1024]{1,0:T(8,128)(2,1)S(1)}, u32[]{:S(2)}, u32[]{:S(2)}) collective-permute-start(bf16[384,1024]{1,0:T(8,128)(2,1)S(1)} %get-tuple-element.92), channel_id=1, source_target_pairs={{0,24},{8,16},{16,8},{24,0},{1,25},{9,17},{17,9},{25,1},{2,26},{10... | collective-permute-start | bytes 2359304 | tf_op jit(solution)/shard_map/ppermute | solution.py:63
  57.3 35.2 %collective-permute-start.1 = (bf16[384,1024]{1,0:T(8,128)(2,1)S(1)}, bf16[384,1024]{1,0:T(8,128)(2,1)}, u32[]{:S(2)}, u32[]{:S(2)}) collective-permute-start(bf16[384,1024]{1,0:T(8,128)(2,1)S(1)} %get-tuple-element.93), channel_id=1, source_target_pairs={{0,16},{8,24},{16,0},{24,8},{1,17},{9,25},{17,1},{25,9},{2,18},{10... | collective-permute-start | bytes 2359304 | tf_op jit(solution)/shard_map/ppermute | solution.py:63
  57.8 34.7 %collective-permute-start = (bf16[384,1024]{1,0:T(8,128)(2,1)S(1)}, bf16[384,1024]{1,0:T(8,128)(2,1)}, u32[]{:S(2)}, u32[]{:S(2)}) collective-permute-start(bf16[384,1024]{1,0:T(8,128)(2,1)S(1)} %get-tuple-element.94), channel_id=1, source_target_pairs={{0,8},{8,0},{16,24},{24,16},{1,9},{9,1},{17,25},{25,17},{2,10},{10... | collective-permute-start | bytes 2359304 | tf_op jit(solution)/shard_map/ppermute | solution.py:63
  93.9 8.0 %collective-permute-start.5 = (bf16[48,1024]{1,0:T(8,128)(2,1)S(1)}, bf16[48,1024]{1,0:T(8,128)(2,1)S(1)}, u32[]{:S(2)}, u32[]{:S(2)}) collective-permute-start(bf16[48,1024]{1,0:T(8,128)(2,1)S(1)} %get-tuple-element.96), channel_id=1, source_target_pairs={{0,24},{8,16},{16,8},{24,0},{1,25},{9,17},{17,9},{25,1},{2,26},{10... | collective-permute-start | bytes 294920 | tf_op jit(solution)/shard_map/ppermute | solution.py:63
  95.6 6.3 %collective-permute-start.4 = (bf16[48,1024]{1,0:T(8,128)(2,1)S(1)}, bf16[48,1024]{1,0:T(8,128)(2,1)S(1)}, u32[]{:S(2)}, u32[]{:S(2)}) collective-permute-start(bf16[48,1024]{1,0:T(8,128)(2,1)S(1)} %get-tuple-element.97), channel_id=1, source_target_pairs={{0,16},{8,24},{16,0},{24,8},{1,17},{9,25},{17,1},{25,9},{2,18},{10... | collective-permute-start | bytes 294920 | tf_op jit(solution)/shard_map/ppermute | solution.py:63
  96.9 5.0 %collective-permute-start.3 = (bf16[48,1024]{1,0:T(8,128)(2,1)S(1)}, bf16[48,1024]{1,0:T(8,128)(2,1)S(1)}, u32[]{:S(2)}, u32[]{:S(2)}) collective-permute-start(bf16[48,1024]{1,0:T(8,128)(2,1)S(1)} %get-tuple-element.98), channel_id=1, source_target_pairs={{0,8},{8,0},{16,24},{24,16},{1,9},{9,1},{17,25},{25,17},{2,10},{10... | collective-permute-start | bytes 294920 | tf_op jit(solution)/shard_map/ppermute | solution.py:63
  102.7 135.5 %reduce-scatter.3.cloned.1.call-start = ((), (), s32[]{:S(2)}) async-start(), calls=%async_computation.5 | async-start | bytes 3538944 | tf_op jit(solution)/shard_map/reduce_scatter | solution.py:117
  125.0 31.7 %collective-permute-start.7 = (bf16[384,1792]{1,0:T(8,128)(2,1)S(1)}, bf16[384,1792]{1,0:T(8,128)(2,1)}, u32[]{:S(2)}, u32[]{:S(2)}) collective-permute-start(bf16[384,1792]{1,0:T(8,128)(2,1)S(1)} %get-tuple-element.53), channel_id=1, source_target_pairs={{0,16},{8,24},{16,0},{24,8},{1,17},{9,25},{17,1},{25,9},{2,18},{10... | collective-permute-start | bytes 4128776 | tf_op jit(solution)/shard_map/ppermute | solution.py:63
  126.5 31.7 %collective-permute-start.6 = (bf16[384,1792]{1,0:T(8,128)(2,1)S(1)}, bf16[384,1792]{1,0:T(8,128)(2,1)}, u32[]{:S(2)}, u32[]{:S(2)}) collective-permute-start(bf16[384,1792]{1,0:T(8,128)(2,1)S(1)} %get-tuple-element.53), channel_id=1, source_target_pairs={{0,8},{8,0},{16,24},{24,16},{1,9},{9,1},{17,25},{25,17},{2,10},{10... | collective-permute-start | bytes 4128776 | tf_op jit(solution)/shard_map/ppermute | solution.py:63
  158.2 133.9 %reduce-scatter.5.cloned.1.call-start = ((), (), s32[]{:S(2)}) async-start(), calls=%async_computation.6 | async-start | bytes 3538944 | tf_op jit(solution)/shard_map/reduce_scatter | solution.py:117
  158.3 46.0 %collective-permute-start.9 = (bf16[384,1792]{1,0:T(8,128)(2,1)}, bf16[384,1792]{1,0:T(8,128)(2,1)}, u32[]{:S(2)}, u32[]{:S(2)}) collective-permute-start(bf16[384,1792]{1,0:T(8,128)(2,1)} %get-tuple-element.49), channel_id=1, source_target_pairs={{0,16},{8,24},{16,0},{24,8},{1,17},{9,25},{17,1},{25,9},{2,18},{10... | collective-permute-start | bytes 4128776 | tf_op jit(solution)/shard_map/ppermute | solution.py:63
  158.6 45.7 %collective-permute-start.8 = (bf16[384,1792]{1,0:T(8,128)(2,1)}, bf16[384,1792]{1,0:T(8,128)(2,1)}, u32[]{:S(2)}, u32[]{:S(2)}) collective-permute-start(bf16[384,1792]{1,0:T(8,128)(2,1)} %get-tuple-element.49), channel_id=1, source_target_pairs={{0,8},{8,0},{16,24},{24,16},{1,9},{9,1},{17,25},{25,17},{2,10},{10... | collective-permute-start | bytes 4128776 | tf_op jit(solution)/shard_map/ppermute | solution.py:63
  164.3 40.0 %collective-permute-start.11 = (bf16[192,1792]{1,0:T(8,128)(2,1)}, bf16[192,1792]{1,0:T(8,128)(2,1)}, u32[]{:S(2)}, u32[]{:S(2)}) collective-permute-start(bf16[192,1792]{1,0:T(8,128)(2,1)} %slice.39), channel_id=1, source_target_pairs={{0,8},{8,0},{16,24},{24,16},{1,9},{9,1},{17,25},{25,17},{2,10},{10... | collective-permute-start | bytes 2064392 | tf_op jit(solution)/shard_map/ppermute | solution.py:63
  164.7 39.6 %collective-permute-start.10 = (bf16[192,1792]{1,0:T(8,128)(2,1)}, bf16[192,1792]{1,0:T(8,128)(2,1)}, u32[]{:S(2)}, u32[]{:S(2)}) collective-permute-start(bf16[192,1792]{1,0:T(8,128)(2,1)} %slice.38), channel_id=1, source_target_pairs={{0,16},{8,24},{16,0},{24,8},{1,17},{9,25},{17,1},{25,9},{2,18},{10... | collective-permute-start | bytes 2064392 | tf_op jit(solution)/shard_map/ppermute | solution.py:63
  208.3 31.1 %collective-permute-start.13 = (bf16[192,1792]{1,0:T(8,128)(2,1)}, bf16[192,1792]{1,0:T(8,128)(2,1)}, u32[]{:S(2)}, u32[]{:S(2)}) collective-permute-start(bf16[192,1792]{1,0:T(8,128)(2,1)} %slice.41), channel_id=1, source_target_pairs={{0,8},{8,0},{16,24},{24,16},{1,9},{9,1},{17,25},{25,17},{2,10},{10... | collective-permute-start | bytes 2064392 | tf_op jit(solution)/shard_map/ppermute | solution.py:63
  209.7 29.7 %collective-permute-start.12 = (bf16[192,1792]{1,0:T(8,128)(2,1)}, bf16[192,1792]{1,0:T(8,128)(2,1)}, u32[]{:S(2)}, u32[]{:S(2)}) collective-permute-start(bf16[192,1792]{1,0:T(8,128)(2,1)} %slice.40), channel_id=1, source_target_pairs={{0,16},{8,24},{16,0},{24,8},{1,17},{9,25},{17,1},{25,9},{2,18},{10... | collective-permute-start | bytes 2064392 | tf_op jit(solution)/shard_map/ppermute | solution.py:63
  239.5 29.3 %collective-permute-start.15 = (bf16[384,1792]{1,0:T(8,128)(2,1)S(1)}, bf16[384,1792]{1,0:T(8,128)(2,1)S(1)}, u32[]{:S(2)}, u32[]{:S(2)}) collective-permute-start(bf16[384,1792]{1,0:T(8,128)(2,1)S(1)} %get-tuple-element.73), channel_id=1, source_target_pairs={{0,16},{8,24},{16,0},{24,8},{1,17},{9,25},{17,1},{25,9},{2,18},{10... | collective-permute-start | bytes 4128776 | tf_op jit(solution)/shard_map/ppermute | solution.py:63
  241.0 30.2 %collective-permute-start.14 = (bf16[384,1792]{1,0:T(8,128)(2,1)S(1)}, bf16[384,1792]{1,0:T(8,128)(2,1)S(1)}, u32[]{:S(2)}, u32[]{:S(2)}) collective-permute-start(bf16[384,1792]{1,0:T(8,128)(2,1)S(1)} %get-tuple-element.73), channel_id=1, source_target_pairs={{0,8},{8,0},{16,24},{24,16},{1,9},{9,1},{17,25},{25,17},{2,10},{10... | collective-permute-start | bytes 4128776 | tf_op jit(solution)/shard_map/ppermute | solution.py:63
  271.3 12.9 %collective-permute-start.17 = (bf16[192,1792]{1,0:T(8,128)(2,1)S(1)}, bf16[192,1792]{1,0:T(8,128)(2,1)S(1)}, u32[]{:S(2)}, u32[]{:S(2)}) collective-permute-start(bf16[192,1792]{1,0:T(8,128)(2,1)S(1)} %slice.43), channel_id=1, source_target_pairs={{0,8},{8,0},{16,24},{24,16},{1,9},{9,1},{17,25},{25,17},{2,10},{10... | collective-permute-start | bytes 2064392 | tf_op jit(solution)/shard_map/ppermute | solution.py:63
  272.2 12.0 %collective-permute-start.16 = (bf16[192,1792]{1,0:T(8,128)(2,1)S(1)}, bf16[192,1792]{1,0:T(8,128)(2,1)S(1)}, u32[]{:S(2)}, u32[]{:S(2)}) collective-permute-start(bf16[192,1792]{1,0:T(8,128)(2,1)S(1)} %slice.42), channel_id=1, source_target_pairs={{0,16},{8,24},{16,0},{24,8},{1,17},{9,25},{17,1},{25,9},{2,18},{10... | collective-permute-start | bytes 2064392 | tf_op jit(solution)/shard_map/ppermute | solution.py:63
  (29 other events, 506.3 us)
Sparse Core Ops, SparseCore 0:
  9.7 40.9 all-gather.4
  52.9 37.1 all-gather.6
  102.9 36.5 all-gather.8
  158.3 38.2 reduce-scatter.2
  222.3 38.3 reduce-scatter.4
